TPU v7x, 512 devices: a whole 4x8x8 slice. The times are simulated.
512 devices in a mesh: replica: 64 (over x, y, core), tensor: 8 (over z).
Axes of the slice: x: 4, y: 8, z: 8, core: 2. Of those that a mesh axis runs over, the one named last changes fastest.
Arguments:
- hidden: bfloat16 [65536, 8192], P('replica', 'tensor'), may hold values from -250 to 250
- norm_gain: bfloat16 [8192], P('tensor'), may hold values from 0.099609375 to 1.8984375
- layer_weight: bfloat16 [64, 8192, 1024], P('replica', 'tensor'), may hold values from -0.0625 to 0.0625
- layer_bias: bfloat16 [64, 1024], P('replica', 'tensor'), may hold values from -3 to 3
- lengths: int32 [64], replicated, may hold values from 1 to 1024, 32768 in all
Outputs:
- keys: bfloat16 [65536, 1024], P('replica', 'tensor')
Inputs may be any that keep to these rules, and one draw needn't show every extreme that they name: Replica r's prompt fills the first lengths[r] rows of its block; some replica's prompt fills its whole block.
All inputs are finite; a program needn't handle non-finite values.
Results may differ from a plain program's by a relative error of at most 0.0046.
Values may be sent and summed in bfloat16 or wider, within the bound.
A program may use at most 64 MiB of HBM per device.

v0:
```python
import jax
import jax.numpy as jnp
from jax import lax
from jax.sharding import PartitionSpec as P

HEAD = 128
GROUP = 4


epsilon = 1e-06
rope_base = 1000000.0


def shifted(block, axis, distance):
    devices = range(lax.axis_size(axis))
    route = [(i - distance, i) for i in devices if i - distance in devices]
    return lax.ppermute(block, axis, route)


def rotate(projected, positions):
    row_count = projected.shape[0]
    per_head = projected.reshape(row_count, -1, HEAD)
    half_size = HEAD // 2
    frequency = 1.0 / rope_base ** (jnp.arange(half_size, dtype=jnp.float32) * (2.0 / HEAD))
    angles = positions[:, None] * frequency[None, :]
    cosine = jnp.cos(angles)[:, None, :]
    sine_part = jnp.sin(angles)[:, None, :]
    first_half = per_head[..., :half_size]
    second = per_head[..., half_size:]
    rotated = jnp.concatenate(
        [first_half * cosine - second * sine_part, second * cosine + first_half * sine_part],
        axis=-1,
    )
    return rotated.reshape(row_count, -1)


def local(hidden, norm_gain, layer_weight, layer_bias, lengths):
    row_count, local_width = hidden.shape
    full_width = local_width * lax.axis_size("tensor")
    values = hidden.astype(jnp.float32)
    sum_squares = lax.psum(jnp.sum(values * values, axis=1), "tensor")
    inverse_rms = lax.rsqrt(sum_squares / full_width + epsilon)
    normed = (values * inverse_rms[:, None] * norm_gain.astype(jnp.float32)[None, :]).astype(
        jnp.bfloat16
    )
    replica_index = lax.axis_index("replica")
    chain_slot = replica_index % GROUP
    weight = layer_weight[0]
    bias_row = layer_bias[0]
    for section in range(1, GROUP):
        incoming = shifted((weight, bias_row), "replica", 1)
        receives = chain_slot == section
        weight = jnp.where(receives, incoming[0], weight)
        bias_row = jnp.where(receives, incoming[1], bias_row)
    own_length = lengths[replica_index]
    partial_sums = jnp.dot(normed, weight, preferred_element_type=jnp.float32)
    key_sums = lax.psum_scatter(partial_sums, "tensor", scatter_dimension=1, tiled=True)
    projected = key_sums + bias_row.astype(jnp.float32)[None, :]
    positions = jnp.arange(row_count, dtype=jnp.int32)
    rotated = rotate(projected, positions.astype(jnp.float32))
    masked = jnp.where((positions < own_length)[:, None], rotated, jnp.float32(0.0))
    return masked.astype(jnp.bfloat16)


def solution(mesh):
    in_specs = (
        P("replica", "tensor"),
        P("tensor"),
        P("replica", "tensor", None),
        P("replica", "tensor"),
        P(),
    )
    out_specs = P("replica", "tensor")
    return jax.shard_map(local, mesh=mesh, in_specs=in_specs, out_specs=out_specs, check_vma=False)
```

profile of v0, /device:TPU:1, one launch (start us, length us, event | category | flops | bytes accessed | tf_op | source)
XLA Modules:
  0.0 178.2 jit_solution(5069754287660169989)
XLA Ops:
  6.5 0.0 reduce-scatter.2.cloned.1.call-start
  6.5 4.6 %collective-permute-start = (bf16[1024,1024]{1,0:T(8,128)(2,1)}, bf16[1024,1024]{1,0:T(8,128)(2,1)}, u32[]{:S(2)}, u32[]{:S(2)}) collective-permute-start(bf16[1024,1024]{1,0:T(8,128)(2,1)} %bitcast.13), channel_id=1, source_target_pairs={{0,8},{8,16},{16,24},{24,32},{32,40},{40,48},{48,56},{56,64},{64,7... | collective-permute-start | bytes 6291464 | tf_op jit(solution)/shard_map/ppermute | solution.py:17
  11.1 23.3 %collective-permute-done = bf16[1024,1024]{1,0:T(8,128)(2,1)} collective-permute-done((bf16[1024,1024]{1,0:T(8,128)(2,1)}, bf16[1024,1024]{1,0:T(8,128)(2,1)}, u32[]{:S(2)}, u32[]{:S(2)}) %collective-permute-start) | collective-permute-done | bytes 2097184 | tf_op jit(solution)/shard_map/ppermute | solution.py:17
  34.4 2.4 %broadcast_select_fusion = bf16[1024,1024]{1,0:T(8,128)(2,1)S(1)} fusion(bf16[1024,1024]{1,0:T(8,128)(2,1)} %collective-permute-done, pred[]{:T(512)S(6)} %eq.13, bf16[1,1024,1024]{2,1,0:T(8,128)(2,1)} %param.7), kind=kLoop, calls=%fused_computation.9 | loop fusion | flops 1048576 | bytes 6291457 | tf_op jit(solution)/shard_map/jit(_where)/select_n | solution.py:53
  36.8 3.8 %collective-permute-start.1 = (bf16[1024,1024]{1,0:T(8,128)(2,1)S(1)}, bf16[1024,1024]{1,0:T(8,128)(2,1)}, u32[]{:S(2)}, u32[]{:S(2)}) collective-permute-start(bf16[1024,1024]{1,0:T(8,128)(2,1)S(1)} %broadcast_select_fusion), channel_id=1, source_target_pairs={{0,8},{8,16},{16,24},{24,32},{32,40},{40,48},{48,56},{56,64},{64,7... | collective-permute-start | bytes 6291464 | tf_op jit(solution)/shard_map/ppermute | solution.py:17
  40.6 0.0 copy-start.1
  40.6 22.9 %collective-permute-done.1 = bf16[1024,1024]{1,0:T(8,128)(2,1)} collective-permute-done((bf16[1024,1024]{1,0:T(8,128)(2,1)S(1)}, bf16[1024,1024]{1,0:T(8,128)(2,1)}, u32[]{:S(2)}, u32[]{:S(2)}) %collective-permute-start.1) | collective-permute-done | bytes 2097184 | tf_op jit(solution)/shard_map/ppermute | solution.py:17
  63.6 1.5 broadcast_select_fusion.1
  65.1 0.0 copy-start
  65.1 6.2 %collective-permute-start.2 = (bf16[1024,1024]{1,0:T(8,128)(2,1)}, bf16[1024,1024]{1,0:T(8,128)(2,1)}, u32[]{:S(2)}, u32[]{:S(2)}) collective-permute-start(bf16[1024,1024]{1,0:T(8,128)(2,1)} %broadcast_select_fusion.1), channel_id=1, source_target_pairs={{0,8},{8,16},{16,24},{24,32},{32,40},{40,48},{48,56},{56,64},{64,7... | collective-permute-start | bytes 6291464 | tf_op jit(solution)/shard_map/ppermute | solution.py:17
  71.3 0.0 copy-done.1
  71.3 2.1 %fusion = f32[1024]{0:T(1024)S(1)} fusion(bf16[1024,1024]{1,0:T(8,128)(2,1)} %param.5), kind=kLoop, calls=%fused_computation.2 | loop fusion | flops 3144704 | bytes 2101248 | tf_op jit(solution)/shard_map/reduce_sum | solution.py:41
  73.4 19.6 %psum.7 = f32[1024]{0:T(1024)S(1)} all-reduce(f32[1024]{0:T(1024)S(1)} %fusion), channel_id=1, replica_groups=mesh['replica'=64,'tensor'=8] {'tensor'}, use_global_device_ids=true, to_apply=%region_1.0 | all-reduce | flops 1024 | bytes 8192 | tf_op jit(solution)/shard_map/psum | solution.py:41
  93.0 1.6 collective-permute-done.2
  94.6 0.0 copy-done
  94.6 5.9 %fusion.3 = f32[1024,1024]{1,0:T(8,128)} fusion(bf16[1024,1024]{1,0:T(8,128)(2,1)S(1)} %copy-done, bf16[1024,1024]{1,0:T(8,128)(2,1)} %collective-permute-done.2, bf16[1024,1024]{1,0:T(8,128)(2,1)} %broadcast_select_fusion.1, f32[1024]{0:T(1024)S(1)} %convert_element_type.29, f32[1024]{0:T(1024)S(1)} %add_rsqrt_fusion, pred[]{:T(512)S(6)} %eq.11), kind=kOutput, calls=%fused_computation.5 | convolution fusion | flops 2152726528 | bytes 10493953 | tf_op jit(solution)/shard_map/dot_general | solution.py:56
  100.5 0.0 copy-start.2
  100.5 0.0 copy-start.3
  100.5 0.0 reduce-scatter.2.cloned.1.call-update
  100.5 0.6 copy-done.2
  101.2 4.4 %collective-permute-start.3 = (bf16[128]{0:T(256)(128)(2,1)S(1)}, bf16[128]{0:T(256)(128)(2,1)S(1)}, u32[]{:S(2)}, u32[]{:S(2)}) collective-permute-start(bf16[128]{0:T(256)(128)(2,1)S(1)} %bitcast.14), channel_id=1, source_target_pairs={{0,8},{8,16},{16,24},{24,32},{32,40},{40,48},{48,56},{56,64},{64,7... | collective-permute-start | bytes 776 | tf_op jit(solution)/shard_map/ppermute | solution.py:17
  105.6 0.0 copy-done.3
  105.6 0.6 dynamic_slice.3
  106.2 0.1 collective-permute-done.3
  106.3 4.1 %collective-permute-start.4 = (bf16[128]{0:T(256)(128)(2,1)S(1)}, bf16[128]{0:T(256)(128)(2,1)S(1)}, u32[]{:S(2)}, u32[]{:S(2)}) collective-permute-start(bf16[128]{0:T(256)(128)(2,1)S(1)} %broadcast_select_fusion.2), channel_id=1, source_target_pairs={{0,8},{8,16},{16,24},{24,32},{32,40},{40,48},{48,56},{56,64},{64,7... | collective-permute-start | bytes 776 | tf_op jit(solution)/shard_map/ppermute | solution.py:17
  110.4 0.7 iota_compare_fusion
  111.1 0.0 collective-permute-done.4
  111.1 4.1 %collective-permute-start.5 = (bf16[128]{0:T(256)(128)(2,1)S(1)}, bf16[128]{0:T(256)(128)(2,1)S(1)}, u32[]{:S(2)}, u32[]{:S(2)}) collective-permute-start(bf16[128]{0:T(256)(128)(2,1)S(1)} %broadcast_select_fusion.3), channel_id=1, source_target_pairs={{0,8},{8,16},{16,24},{24,32},{32,40},{40,48},{48,56},{56,64},{64,7... | collective-permute-start | bytes 776 | tf_op jit(solution)/shard_map/ppermute | solution.py:17
  115.3 0.7 collective-permute-done.5
  116.0 50.8 %reduce-scatter.2.cloned.1.call-done = f32[1024,128]{1,0:T(8,128)} async-done(((f32[1024,1024]{1,0:T(8,128)}), f32[1024,128]{1,0:T(8,128)}) %reduce-scatter.2.cloned.1.call-update) | async-done | bytes 524304 | tf_op jit(solution)/shard_map/reduce_scatter | solution.py:57
  166.8 1.1 add_bitcast_fusion
  167.9 2.4 %fusion.13 = (bf16[1024,1,64]{2,0,1:T(8,128)(2,1)S(1)}, bf16[1024,1,64]{2,0,1:T(8,128)(2,1)S(1)}) fusion(f32[1024,1,128]{2,0,1:T(8,128)S(1)} %add_bitcast_fusion, f32[64]{0:T(128)S(1)} %negate_power_fusion, f32[1024]{0:T(1024)S(1)} %iota_convert_fusion), kind=kLoop, calls=%fused_computation.18 | loop fusion | flops 589824 | bytes 790784 | tf_op jit(solution)/shard_map/sub | solution.py:31
  170.3 1.0 fusion.16
  (7 shorter events, 0.0 us)
Async XLA Ops:
  6.5 160.3 %reduce-scatter.2.cloned.1.call-start = ((), (), s32[]{:S(2)}) async-start(), calls=%async_computation.1 | async-start | bytes 4718592 | tf_op jit(solution)/shard_map/reduce_scatter | solution.py:57
  6.5 27.9 %collective-permute-start = (bf16[1024,1024]{1,0:T(8,128)(2,1)}, bf16[1024,1024]{1,0:T(8,128)(2,1)}, u32[]{:S(2)}, u32[]{:S(2)}) collective-permute-start(bf16[1024,1024]{1,0:T(8,128)(2,1)} %bitcast.13), channel_id=1, source_target_pairs={{0,8},{8,16},{16,24},{24,32},{32,40},{40,48},{48,56},{56,64},{64,7... | collective-permute-start | bytes 6291464 | tf_op jit(solution)/shard_map/ppermute | solution.py:17
  36.8 26.7 %collective-permute-start.1 = (bf16[1024,1024]{1,0:T(8,128)(2,1)S(1)}, bf16[1024,1024]{1,0:T(8,128)(2,1)}, u32[]{:S(2)}, u32[]{:S(2)}) collective-permute-start(bf16[1024,1024]{1,0:T(8,128)(2,1)S(1)} %broadcast_select_fusion), channel_id=1, source_target_pairs={{0,8},{8,16},{16,24},{24,32},{32,40},{40,48},{48,56},{56,64},{64,7... | collective-permute-start | bytes 6291464 | tf_op jit(solution)/shard_map/ppermute | solution.py:17
  40.6 30.7 %copy-start.1 = (bf16[1024]{0:T(1024)(128)(2,1)S(1)}, bf16[1024]{0:T(1024)(128)(2,1)}, u32[]{:S(2)}) copy-start(bf16[1024]{0:T(1024)(128)(2,1)} %param.6) | copy-start | bytes 6148
  65.1 29.5 %copy-start = (bf16[1024,1024]{1,0:T(8,128)(2,1)S(1)}, bf16[1024,1024]{1,0:T(8,128)(2,1)}, u32[]{:S(2)}) copy-start(bf16[1024,1024]{1,0:T(8,128)(2,1)} %param.5) | copy-start | bytes 6291460
  65.1 29.5 %collective-permute-start.2 = (bf16[1024,1024]{1,0:T(8,128)(2,1)}, bf16[1024,1024]{1,0:T(8,128)(2,1)}, u32[]{:S(2)}, u32[]{:S(2)}) collective-permute-start(bf16[1024,1024]{1,0:T(8,128)(2,1)} %broadcast_select_fusion.1), channel_id=1, source_target_pairs={{0,8},{8,16},{16,24},{24,32},{32,40},{40,48},{48,56},{56,64},{64,7... | collective-permute-start | bytes 6291464 | tf_op jit(solution)/shard_map/ppermute | solution.py:17
  100.5 0.7 copy-start.2
  100.5 5.0 %copy-start.3 = (s32[64]{0:T(128)S(1)}, s32[64]{0:T(128)}, u32[]{:S(2)}) copy-start(s32[64]{0:T(128)} %param.9) | copy-start | bytes 772
  101.2 5.1 %collective-permute-start.3 = (bf16[128]{0:T(256)(128)(2,1)S(1)}, bf16[128]{0:T(256)(128)(2,1)S(1)}, u32[]{:S(2)}, u32[]{:S(2)}) collective-permute-start(bf16[128]{0:T(256)(128)(2,1)S(1)} %bitcast.14), channel_id=1, source_target_pairs={{0,8},{8,16},{16,24},{24,32},{32,40},{40,48},{48,56},{56,64},{64,7... | collective-permute-start | bytes 776 | tf_op jit(solution)/shard_map/ppermute | solution.py:17
  106.3 4.8 %collective-permute-start.4 = (bf16[128]{0:T(256)(128)(2,1)S(1)}, bf16[128]{0:T(256)(128)(2,1)S(1)}, u32[]{:S(2)}, u32[]{:S(2)}) collective-permute-start(bf16[128]{0:T(256)(128)(2,1)S(1)} %broadcast_select_fusion.2), channel_id=1, source_target_pairs={{0,8},{8,16},{16,24},{24,32},{32,40},{40,48},{48,56},{56,64},{64,7... | collective-permute-start | bytes 776 | tf_op jit(solution)/shard_map/ppermute | solution.py:17
  111.1 4.8 %collective-permute-start.5 = (bf16[128]{0:T(256)(128)(2,1)S(1)}, bf16[128]{0:T(256)(128)(2,1)S(1)}, u32[]{:S(2)}, u32[]{:S(2)}) collective-permute-start(bf16[128]{0:T(256)(128)(2,1)S(1)} %broadcast_select_fusion.3), channel_id=1, source_target_pairs={{0,8},{8,16},{16,24},{24,32},{32,40},{40,48},{48,56},{56,64},{64,7... | collective-permute-start | bytes 776 | tf_op jit(solution)/shard_map/ppermute | solution.py:17
Sparse Core Ops, SparseCore 0:
  100.7 66.1 reduce-scatter.1
where the time goes:
time: 179 us; the launch traced here: 178 us
  waiting for transfers between devices  99.4 us (56%)
  starting transfers between devices  27.2 us (15%)
  blocking collectives  19.6 us (11%)
  between operations  13.5 us (8%)
  other arithmetic  11.2 us (6%)
  matrix products  5.92 us (3%)
    reduce_scatter x1, waiting for transfers between devices, local(): lax.psum_scatter(partial_sums, 'tensor', scatter_dimension=1, tiled=True)  50.8 us
    ppermute x6, waiting for transfers between devices, shifted(): return lax.ppermute(block, axis, route)  48.6 us
    ppermute x6, starting transfers between devices, shifted(): return lax.ppermute(block, axis, route)  27.2 us
    psum x1, blocking collectives, local(): sum_squares = lax.psum(jnp.sum(values * values, axis=1), 'tensor')  19.6 us
    dot_general x1, matrix products, local(): partial_sums = jnp.dot(normed, weight, preferred_element_type=jnp.float32)  5.92 us
    select_n x2, other arithmetic, local(): weight = jnp.where(receives, incoming[0], weight)  3.98 us
  transfers between devices with their start and end apart: 7, of which 6 were waited for; matrix products, arithmetic and copies ran while one was open for 2% of the time, Pallas kernels for 0%

commit v1 on v0

v1 whole, which is shorter than its diff:
```python
import functools

import jax
import jax.numpy as jnp
import numpy as np
from jax import lax
from jax.experimental import pallas as pl
from jax.experimental.pallas import tpu as pltpu
from jax.sharding import PartitionSpec as P

HEAD = 128
GROUP = 4
SUB = 256
EPSILON = 1e-06
ROPE_BASE = 1000000.0
MESH = pl.DeviceIdType.MESH


def rope_table(rows):
    half = HEAD // 2
    exponent = np.arange(half, dtype=np.float32) * np.float32(2.0 / HEAD)
    frequency = np.float32(1.0) / np.power(np.float32(ROPE_BASE), exponent)
    angles = np.arange(rows, dtype=np.float32)[:, None] * frequency[None, :]
    angles = angles.astype(np.float64)
    return np.concatenate([np.cos(angles), np.sin(angles)], axis=1).astype(np.float32)


def kernel(
    ring,
    hid, gain, weight, bias, lens, table,
    out,
    h_v, n_v, w_v, t_v, squares, bias_v, send_v, recv_v,
    h_sem, t_sem, w_sem, head_send, half_recv, swap_send, swap_recv,
    square_send, square_recv, bias_send, bias_recv, ring_send, ring_recv,
):
    rows, depth = h_v.shape
    subs = rows // SUB
    half_rows = depth // 2
    replica = lax.axis_index("replica")
    z = lax.axis_index("tensor")
    slot = lax.rem(replica, GROUP)
    head = replica - slot
    partner = head + 2 + (1 - lax.rem(slot, 2))

    def at(distance):
        return lax.rem(z + (distance + ring), ring)

    order = [ring // 2]
    for distance in range(ring // 2 - 1, 0, -1):
        order += [distance, -distance]
    order += [0]

    def columns(distance):
        return pl.ds(pl.multiple_of(at(distance) * HEAD, HEAD), HEAD)

    barrier = pltpu.get_barrier_semaphore()
    for distance in range(1, ring):
        pl.semaphore_signal(barrier, inc=1, device_id={"tensor": at(distance)}, device_id_type=MESH)
    for step in range(1, GROUP):
        other = head + lax.rem(slot + step, GROUP)
        pl.semaphore_signal(barrier, inc=1, device_id={"replica": other}, device_id_type=MESH)

    def load_hidden(block):
        part = pl.ds(block * SUB, SUB)
        return pltpu.make_async_copy(hid.at[part], h_v.at[part], h_sem.at[block])

    def load_weight(i):
        return pltpu.make_async_copy(weight.at[0, :, columns(order[i])], w_v.at[i], w_sem.at[i])

    load_table = pltpu.make_async_copy(table, t_v, t_sem)

    @pl.when(slot == 0)
    def _():
        for i in range(ring):
            load_weight(i).start()

    for block in range(subs):
        load_hidden(block).start()
    load_table.start()

    pl.semaphore_wait(barrier, ring - 1 + GROUP - 1)

    low, high = pl.ds(0, half_rows), pl.ds(half_rows, half_rows)

    def head_copies(i):
        whole = pltpu.make_async_remote_copy(
            src_ref=w_v.at[i], dst_ref=w_v.at[i],
            send_sem=head_send.at[i, 0], recv_sem=w_sem.at[i],
            device_id={"replica": head + 1}, device_id_type=MESH)
        halves = [
            pltpu.make_async_remote_copy(
                src_ref=w_v.at[i, part], dst_ref=w_v.at[i, part],
                send_sem=head_send.at[i, 1 + core], recv_sem=half_recv.at[i],
                device_id={"replica": head + 2 + core}, device_id_type=MESH)
            for core, part in enumerate((low, high))
        ]
        return halves + [whole]

    def bias_copies():
        return [
            pltpu.make_async_remote_copy(
                src_ref=bias_v, dst_ref=bias_v,
                send_sem=bias_send.at[step], recv_sem=bias_recv,
                device_id={"replica": head + step}, device_id_type=MESH)
            for step in range(1, GROUP)
        ]

    @pl.when(slot == 0)
    def _():
        for i in range(ring):
            load_weight(i).wait()
            for copy in head_copies(i):
                copy.start()
        bias_v[...] = jnp.broadcast_to(bias[...], bias_v.shape)
        for copy in bias_copies():
            copy.start()

    for block in range(subs):
        load_hidden(block).wait()
        for i in range(block * SUB // HEAD, (block + 1) * SUB // HEAD):
            values = h_v[pl.ds(i * HEAD, HEAD), :].astype(jnp.float32)
            total = jnp.zeros((HEAD, HEAD), jnp.float32)
            for j in range(depth // HEAD):
                piece = values[:, j * HEAD:(j + 1) * HEAD]
                total = total + piece * piece
            squares[0, pl.ds(i, 1), :] = jnp.sum(total.T, axis=0, keepdims=True)

    def square_copy(distance):
        return pltpu.make_async_remote_copy(
            src_ref=squares.at[0], dst_ref=squares.at[distance],
            send_sem=square_send.at[distance], recv_sem=square_recv.at[distance],
            device_id={"tensor": at(distance)}, device_id_type=MESH)

    for distance in range(1, ring):
        square_copy(distance).start()
    for distance in range(1, ring):
        square_copy(distance).wait_recv()

    sums = squares[0]
    for distance in range(1, ring):
        sums = sums + squares[distance]
    inverse = lax.rsqrt(sums / (depth * ring) + EPSILON)
    gain_row = gain[...].astype(jnp.float32)
    for i in range(rows // HEAD):
        part = pl.ds(i * HEAD, HEAD)
        scale = jnp.broadcast_to(inverse[i:i + 1, :], (HEAD, HEAD)).T
        for j in range(depth // HEAD):
            cols = pl.ds(j * HEAD, HEAD)
            values = h_v[part, cols].astype(jnp.float32)
            n_v[part, cols] = (values * scale * gain_row[:, j * HEAD:(j + 1) * HEAD]).astype(jnp.bfloat16)

    def swap_copy(i, part, to):
        return pltpu.make_async_remote_copy(
            src_ref=w_v.at[i, part], dst_ref=w_v.at[i, part],
            send_sem=swap_send.at[i], recv_sem=swap_recv.at[i],
            device_id={"replica": to}, device_id_type=MESH)

    def take_weight(i):
        @pl.when(slot == 1)
        def _():
            pltpu.make_async_remote_copy(
                src_ref=w_v.at[i], dst_ref=w_v.at[i],
                send_sem=head_send.at[i, 0], recv_sem=w_sem.at[i],
                device_id={"replica": head + 1}, device_id_type=MESH).wait_recv()

        for core, (mine, theirs) in enumerate(((low, high), (high, low))):
            @pl.when(slot == 2 + core)
            def _():
                pltpu.make_async_remote_copy(
                    src_ref=w_v.at[i, mine], dst_ref=w_v.at[i, mine],
                    send_sem=head_send.at[i, 1 + core], recv_sem=half_recv.at[i],
                    device_id={"replica": head}, device_id_type=MESH).wait_recv()
                swap_copy(i, mine, partner).start()
                swap_copy(i, theirs, partner).wait_recv()

    def product(i, sub):
        return jnp.dot(n_v[pl.ds(sub * SUB, SUB), :], w_v[i], preferred_element_type=jnp.float32)

    def hop(distance, positive):
        return (abs(distance) - 1) + (0 if positive else ring // 2)

    def ring_copy(distance, positive, sub):
        h = hop(distance, positive)
        part = pl.ds(sub * SUB, SUB)
        return pltpu.make_async_remote_copy(
            src_ref=send_v.at[h, part], dst_ref=recv_v.at[h, part],
            send_sem=ring_send.at[h, sub], recv_sem=ring_recv.at[h, sub],
            device_id={"tensor": at(1 if positive else -1)}, device_id_type=MESH)

    def incoming(distance, positive, sub):
        ring_copy(distance, positive, sub).wait_recv()
        return recv_v[hop(distance, positive), pl.ds(sub * SUB, SUB)].astype(jnp.float32)

    started = []
    plus_first = [s for s in range(subs) if s < subs // 2]
    minus_first = [s for s in range(subs) if s >= subs // 2]
    for i, distance in enumerate(order[:-1]):
        take_weight(i)
        if distance == ring // 2:
            work = [(True, s) for s in plus_first] + [(False, s) for s in minus_first]
        elif distance > 0:
            work = [(True, s) for s in minus_first + plus_first]
        else:
            work = [(False, s) for s in plus_first + minus_first]
        for positive, sub in work:
            value = product(i, sub)
            step = abs(distance)
            far = step + 1
            first = plus_first if positive else minus_first
            if far < ring // 2 or (far == ring // 2 and sub in first):
                value = value + incoming(far, positive, sub)
            send_v[hop(step, positive), pl.ds(sub * SUB, SUB)] = value.astype(jnp.bfloat16)
            copy = ring_copy(step, positive, sub)
            copy.start()
            started.append(copy)

    last = len(order) - 1
    take_weight(last)
    load_table.wait()

    @pl.when(slot > 0)
    def _():
        pltpu.make_async_remote_copy(
            src_ref=bias_v, dst_ref=bias_v,
            send_sem=bias_send.at[1], recv_sem=bias_recv,
            device_id={"replica": head}, device_id_type=MESH).wait_recv()

    bias_row = bias_v[0:1, :].astype(jnp.float32)
    own_length = lens[replica]
    lane = lax.broadcasted_iota(jnp.int32, (SUB, HEAD), 1)
    row = lax.broadcasted_iota(jnp.int32, (SUB, HEAD), 0)
    in_first = lane < HEAD // 2
    for sub in minus_first + plus_first:
        part = pl.ds(sub * SUB, SUB)
        value = product(last, sub)
        value = value + incoming(1, True, sub)
        value = value + incoming(1, False, sub)
        value = value + bias_row
        trig = t_v[part, :]
        swapped = pltpu.roll(trig, HEAD // 2, 1)
        cosine = jnp.where(in_first, trig, swapped)
        sine = jnp.where(in_first, -swapped, trig)
        rotated = value * cosine + pltpu.roll(value, HEAD // 2, 1) * sine
        kept = jnp.where(row + sub * SUB < own_length, rotated, 0.0)
        out[part, :] = kept.astype(jnp.bfloat16)

    for copy in started:
        copy.wait_send()
    for distance in range(1, ring):
        square_copy(distance).wait_send()

    @pl.when(slot == 0)
    def _():
        for i in range(ring):
            for copy in head_copies(i):
                copy.wait_send()
        for copy in bias_copies():
            copy.wait_send()

    for core, mine in enumerate((low, high)):
        @pl.when(slot == 2 + core)
        def _():
            for i in range(ring):
                swap_copy(i, mine, partner).wait_send()


def solution(mesh):
    ring = mesh.shape["tensor"]

    def local(hidden, norm_gain, layer_weight, layer_bias, lengths):
        rows, depth = hidden.shape
        subs = rows // SUB
        table = jnp.asarray(rope_table(rows))
        vmem = pl.BlockSpec(memory_space=pltpu.VMEM)
        hbm = pl.BlockSpec(memory_space=pl.ANY)
        dma = pltpu.SemaphoreType.DMA
        return pl.pallas_call(
            functools.partial(kernel, ring),
            out_shape=jax.ShapeDtypeStruct((rows, HEAD), jnp.bfloat16),
            in_specs=[hbm, vmem, hbm, vmem, pl.BlockSpec(memory_space=pltpu.SMEM), hbm],
            out_specs=vmem,
            scratch_shapes=[
                pltpu.VMEM((rows, depth), jnp.bfloat16),
                pltpu.VMEM((rows, depth), jnp.bfloat16),
                pltpu.VMEM((ring, depth, HEAD), jnp.bfloat16),
                pltpu.VMEM((rows, HEAD), jnp.float32),
                pltpu.VMEM((ring, rows // HEAD, HEAD), jnp.float32),
                pltpu.VMEM((16, HEAD), jnp.bfloat16),
                pltpu.VMEM((ring, rows, HEAD), jnp.bfloat16),
                pltpu.VMEM((ring, rows, HEAD), jnp.bfloat16),
                dma((subs,)),
                dma,
                dma((ring,)),
                dma((ring, 3)),
                dma((ring,)),
                dma((ring,)),
                dma((ring,)),
                dma((ring,)),
                dma((ring,)),
                dma((GROUP,)),
                dma,
                dma((ring, subs)),
                dma((ring, subs)),
            ],
            compiler_params=pltpu.CompilerParams(
                collective_id=0, has_side_effects=True, vmem_limit_bytes=48 * 1024 * 1024
            ),
            name="keys",
        )(hidden, norm_gain.reshape(1, depth), layer_weight, layer_bias, lengths, table)

    in_specs = (
        P("replica", "tensor"),
        P("tensor"),
        P("replica", "tensor", None),
        P("replica", "tensor"),
        P(),
    )
    return jax.shard_map(
        local, mesh=mesh, in_specs=in_specs, out_specs=P("replica", "tensor"), check_vma=False
    )
```

time: 179 us -> 54.7 us (0.31)
  the two profiles are of different devices: /device:TPU:1 before, /device:TPU:59 now
where the time goes in v1:
time: 54.7 us; the launch traced here: 54.4 us
  Pallas kernels  47.5 us (87%)
  local copies, waits for them, and re-layouts  6.92 us (13%)
    pallas_call x1, Pallas kernels, local(): pl.pallas_call(functools.partial(kernel, ring), out_shape=jax.ShapeDtypeS...  47.5 us
    unnamed x11, local copies, waits for them, and re-layouts  6.24 us

profile of v1, /device:TPU:59, one launch (start us, length us, event | category | flops | bytes accessed | tf_op | source)
XLA Modules:
  0.0 54.4 jit_solution(963539978126805691)
XLA Ops:
  0.0 0.7 %reshape.3.gain = bf16[1,1024]{1,0:T(2,128)(2,1)S(1)} reshape(bf16[1024]{0:T(1024)(128)(2,1)} %param.7) | data formatting | bytes 4096 | tf_op jit(solution)/shard_map/reshape | solution.py:309
  0.7 0.0 copy-start
  0.7 1.6 %copy-done = bf16[1024,1024]{1,0:T(8,128)(2,1)S(1)} copy-done((bf16[1024,1024]{1,0:T(8,128)(2,1)S(1)}, bf16[1024,1024]{1,0:T(8,128)(2,1)}, u32[]{:S(2)}) %copy-start) | copy-done | bytes 2097176
  2.3 0.0 copy-start.1
  2.3 1.6 %copy-done.1 = bf16[1,1024,1024]{2,1,0:T(8,128)(2,1)S(1)} copy-done((bf16[1,1024,1024]{2,1,0:T(8,128)(2,1)S(1)}, bf16[1,1024,1024]{2,1,0:T(8,128)(2,1)}, u32[]{:S(2)}) %copy-start.1) | copy-done | bytes 2097176
  3.9 0.0 copy-start.2
  3.9 1.0 %copy-done.2 = f32[1024,128]{1,0:T(8,128)S(1)} copy-done((f32[1024,128]{1,0:T(8,128)S(1)}, f32[1024,128]{1,0:T(8,128)}, u32[]{:S(2)}) %copy-start.2) | copy-done | bytes 524312
  4.9 0.0 copy-start.3
  4.9 0.7 %copy-done.3 = bf16[1,128]{1,0:T(2,128)(2,1)S(1)} copy-done((bf16[1,128]{1,0:T(2,128)(2,1)S(1)}, bf16[1,128]{1,0:T(2,128)(2,1)}, u32[]{:S(2)}) %copy-start.3) | copy-done | bytes 280
  5.6 0.0 copy-start.4
  5.6 0.7 %copy-done.4 = s32[64]{0:T(128)S(1)} copy-done((s32[64]{0:T(128)S(1)}, s32[64]{0:T(128)}, u32[]{:S(2)}) %copy-start.4) | copy-done | bytes 280
  6.2 47.5 %keys.1 = bf16[1024,128]{1,0:T(8,128)(2,1)S(1)} custom-call(bf16[1024,1024]{1,0:T(8,128)(2,1)S(1)} %copy-done, bf16[1,1024]{1,0:T(2,128)(2,1)S(1)} %reshape.3.gain, bf16[1,1024,1024]{2,1,0:T(8,128)(2,1)S(1)} %copy-done.1, bf16[1,128]{1,0:T(2,128)(2,1)S(1)} %copy-done.3, s32[64]{0:T(128)S(1)} %copy-done.4, f32[1024,128]{1,0:T(8,128)S(1)} %copy-done.2), custom_call_target="tpu_custom_call" | custom-call | tf_op jit(solution)/shard_map/keys/pallas_call | solution.py:277
  53.7 0.7 %copy.8 = bf16[1024,128]{1,0:T(8,128)(2,1)} copy(bf16[1024,128]{1,0:T(8,128)(2,1)S(1)} %keys.1) | data formatting | bytes 524288
Async XLA Ops:
  0.7 1.6 %copy-start = (bf16[1024,1024]{1,0:T(8,128)(2,1)S(1)}, bf16[1024,1024]{1,0:T(8,128)(2,1)}, u32[]{:S(2)}) copy-start(bf16[1024,1024]{1,0:T(8,128)(2,1)} %hid.1) | copy-start | bytes 6291460
  2.3 1.6 %copy-start.1 = (bf16[1,1024,1024]{2,1,0:T(8,128)(2,1)S(1)}, bf16[1,1024,1024]{2,1,0:T(8,128)(2,1)}, u32[]{:S(2)}) copy-start(bf16[1,1024,1024]{2,1,0:T(8,128)(2,1)} %weight.1) | copy-start | bytes 6291460
  3.9 1.0 %copy-start.2 = (f32[1024,128]{1,0:T(8,128)S(1)}, f32[1024,128]{1,0:T(8,128)}, u32[]{:S(2)}) copy-start(f32[1024,128]{1,0:T(8,128)} %constant.2.clone.table) | copy-start | bytes 1572868
  4.9 0.7 %copy-start.3 = (bf16[1,128]{1,0:T(2,128)(2,1)S(1)}, bf16[1,128]{1,0:T(2,128)(2,1)}, u32[]{:S(2)}) copy-start(bf16[1,128]{1,0:T(2,128)(2,1)} %bias.1) | copy-start | bytes 772
  5.6 0.7 %copy-start.4 = (s32[64]{0:T(128)S(1)}, s32[64]{0:T(128)}, u32[]{:S(2)}) copy-start(s32[64]{0:T(128)} %lens.1) | copy-start | bytes 772

commit v2 on v1

v2 whole, which is shorter than its diff:
```python
import functools

import jax
import jax.numpy as jnp
import numpy as np
from jax import lax
from jax.experimental import pallas as pl
from jax.experimental.pallas import tpu as pltpu
from jax.sharding import PartitionSpec as P

HEAD = 128
HALF = HEAD // 2
GROUP = 4
SUB = 512
EPSILON = 1e-06
ROPE_BASE = 1000000.0
MESH = pl.DeviceIdType.MESH


def rope_table(rows):
    exponent = np.arange(HALF, dtype=np.float32) * np.float32(2.0 / HEAD)
    frequency = np.float32(1.0) / np.power(np.float32(ROPE_BASE), exponent)
    angles = np.arange(rows, dtype=np.float32)[:, None] * frequency[None, :]
    angles = angles.astype(np.float64)
    return np.concatenate([np.cos(angles), np.sin(angles)], axis=1).astype(np.float32)


def trade(x, y):
    first = lax.broadcasted_iota(jnp.int32, x.shape, 1) < HALF
    x_other, y_other = pltpu.roll(x, HALF, 1), pltpu.roll(y, HALF, 1)
    return jnp.where(first, x, y_other), jnp.where(first, x_other, y)


def kernel(
    ring,
    hid, gain_h, weight, bias_h, lens_h, table,
    out,
    h_v, n_v, w_n, w_v, t_v, gain, bias, lens, squares, bias_v, send_v, recv_v,
    h_sem, t_sem, small_sem, n_sem, w_sem, head_send, pass_send,
    square_send, square_recv, bias_send, bias_recv, ring_send, ring_recv,
):
    rows, depth = h_v.shape
    subs = rows // SUB
    far = ring // 2
    replica = lax.axis_index("replica")
    z = lax.axis_index("tensor")
    slot = lax.rem(replica, GROUP)
    head = replica - slot

    def at(distance):
        return lax.rem(z + (distance + ring), ring)

    def columns(distance):
        return pl.ds(pl.multiple_of(at(distance) * HEAD, HEAD), HEAD)

    barrier = pltpu.get_barrier_semaphore()
    for step in range(1, GROUP):
        other = head + lax.rem(slot + step, GROUP)
        pl.semaphore_signal(barrier, inc=1, device_id={"replica": other}, device_id_type=MESH)
    for distance in range(1, ring):
        pl.semaphore_signal(barrier, inc=1, device_id={"tensor": at(distance)}, device_id_type=MESH)
    waits = ring - 1 + GROUP - 1

    def load_hidden(block):
        part = pl.ds(block * SUB, SUB)
        return pltpu.make_async_copy(hid.at[part], h_v.at[part], h_sem.at[block])

    last = ring - 1

    def load_whole(i):
        distance = far if i == 0 else 0
        return pltpu.make_async_copy(weight.at[0, :, columns(distance)], w_v.at[i], w_sem.at[i])

    def load_part(k, sign):
        j = 2 * (k - 1) + (0 if sign > 0 else 1)
        return pltpu.make_async_copy(weight.at[0, :, columns(sign * k)], w_n.at[j], n_sem.at[j])

    load_table = pltpu.make_async_copy(table, t_v, t_sem)
    load_gain = pltpu.make_async_copy(gain_h, gain, small_sem.at[0])
    load_bias = pltpu.make_async_copy(bias_h, bias, small_sem.at[1])
    load_lens = pltpu.make_async_copy(lens_h, lens, small_sem.at[2])

    @pl.when(slot == 0)
    def _():
        load_whole(0).start()
        for k in range(far - 1, 0, -1):
            load_part(k, 1).start()
            load_part(k, -1).start()
        load_whole(last).start()

    load_gain.start()
    for block in range(subs):
        load_hidden(block).start()
    load_bias.start()
    load_lens.start()
    load_table.start()

    def block_of(k, half):
        return 1 + 2 * (far - 1 - k) + half

    def mix(k):
        load_part(k, 1).wait()
        load_part(k, -1).wait()
        j = 2 * (k - 1)
        for r in range(0, depth, HEAD):
            part = pl.ds(r, HEAD)
            plus = w_n[j, part].astype(jnp.float32)
            minus = w_n[j + 1, part].astype(jnp.float32)
            for half, mixed in enumerate(trade(plus, minus)):
                w_v[block_of(k, half), part] = mixed.astype(jnp.bfloat16)

    def head_copies(i):
        return [
            pltpu.make_async_remote_copy(
                src_ref=w_v.at[i], dst_ref=w_v.at[i],
                send_sem=head_send.at[i, to - 1], recv_sem=w_sem.at[i],
                device_id={"replica": head + to}, device_id_type=MESH)
            for to in (2, 1)
        ]

    def pass_copy(i):
        return pltpu.make_async_remote_copy(
            src_ref=w_v.at[i], dst_ref=w_v.at[i],
            send_sem=pass_send.at[i], recv_sem=w_sem.at[i],
            device_id={"replica": head + 3}, device_id_type=MESH)

    def bias_copies():
        return [
            pltpu.make_async_remote_copy(
                src_ref=bias_v, dst_ref=bias_v,
                send_sem=bias_send.at[step], recv_sem=bias_recv,
                device_id={"replica": head + step}, device_id_type=MESH)
            for step in range(1, GROUP)
        ]

    def prepare():
        load_gain.wait()
        gain_row = gain[...].astype(jnp.float32).reshape(1, depth)
        for block in range(subs):
            load_hidden(block).wait()
            for i in range(block * SUB // HEAD, (block + 1) * SUB // HEAD):
                part = pl.ds(i * HEAD, HEAD)
                total = jnp.zeros((HEAD, HEAD), jnp.float32)
                for j in range(depth // HEAD):
                    cols = slice(j * HEAD, (j + 1) * HEAD)
                    piece = h_v[part, cols].astype(jnp.float32)
                    total = total + piece * piece
                    n_v[part, cols] = (piece * gain_row[:, cols]).astype(jnp.bfloat16)
                squares[0, pl.ds(i, 1), :] = jnp.sum(total.T, axis=0, keepdims=True)

    @pl.when(slot == 0)
    def _():
        load_whole(0).wait()
        mix(far - 1)
        pl.semaphore_wait(barrier, waits)
        for i in range(ring):
            if i > 2 and i < last and i % 2 == 1:
                mix(far - 1 - i // 2)
            if i == last:
                load_whole(last).wait()
            for copy in head_copies(i):
                copy.start()
        prepare()

    @pl.when(slot > 0)
    def _():
        prepare()
        pl.semaphore_wait(barrier, waits)

    def square_copy(distance):
        return pltpu.make_async_remote_copy(
            src_ref=squares.at[0], dst_ref=squares.at[distance],
            send_sem=square_send.at[distance], recv_sem=square_recv.at[distance],
            device_id={"tensor": at(distance)}, device_id_type=MESH)

    for distance in range(1, ring):
        square_copy(distance).start()
    load_bias.wait()

    @pl.when(slot == 0)
    def _():
        bias_v[...] = jnp.broadcast_to(bias[...], bias_v.shape)
        for copy in bias_copies():
            copy.start()

    def take_weight(i):
        @pl.when(slot > 0)
        def _():
            pass_copy(i).wait_recv()

        @pl.when(slot == 2)
        def _():
            pass_copy(i).start()

    def product(i, sub):
        return jnp.dot(n_v[pl.ds(sub * SUB, SUB), :], w_v[i], preferred_element_type=jnp.float32)

    def ring_copy(distance, positive, half, sub):
        h = (distance - 1) + (0 if positive else far)
        part = pl.ds(sub * SUB // 2, SUB // 2)
        return pltpu.make_async_remote_copy(
            src_ref=send_v.at[h, half, part], dst_ref=recv_v.at[h, half, part],
            send_sem=ring_send.at[h, half, sub], recv_sem=ring_recv.at[h, half, sub],
            device_id={"tensor": at(1 if positive else -1)}, device_id_type=MESH)

    def incoming(distance, positive, half, sub):
        ring_copy(distance, positive, half, sub).wait_recv()
        h = (distance - 1) + (0 if positive else far)
        return recv_v[h, half, pl.ds(sub * SUB // 2, SUB // 2)].astype(jnp.float32)

    started = []

    def forward(distance, positive, half, sub, value):
        h = (distance - 1) + (0 if positive else far)
        send_v[h, half, pl.ds(sub * SUB // 2, SUB // 2)] = value.astype(jnp.bfloat16)
        copy = ring_copy(distance, positive, half, sub)
        copy.start()
        started.append(copy)

    def starts(positive, sub):
        return (sub < subs // 2) == positive

    take_weight(0)
    for sub in range(subs):
        value = product(0, sub)
        for half, packed in enumerate(trade(value[:SUB // 2], value[SUB // 2:])):
            forward(far, starts(True, sub), half, sub, packed)

    for k in range(far - 1, 0, -1):
        for half in (0, 1):
            take_weight(block_of(k, half))
            for sub in range(subs):
                value = product(block_of(k, half), sub)
                plus, minus = trade(value[:SUB // 2], value[SUB // 2:])
                ways = [(True, plus), (False, minus)]
                if k == far - 1 and starts(True, sub):
                    ways = ways[::-1]
                for positive, packed in ways:
                    if k < far - 1 or starts(positive, sub):
                        packed = packed + incoming(k + 1, positive, half, sub)
                    forward(k, positive, half, sub, packed)

    take_weight(last)
    load_table.wait()
    load_lens.wait()
    sums = squares[0]
    for distance in range(1, ring):
        square_copy(distance).wait_recv()
        sums = sums + squares[distance]
    inverse = lax.rsqrt(sums / (depth * ring) + EPSILON)

    @pl.when(slot > 0)
    def _():
        pltpu.make_async_remote_copy(
            src_ref=bias_v, dst_ref=bias_v,
            send_sem=bias_send.at[1], recv_sem=bias_recv,
            device_id={"replica": head}, device_id_type=MESH).wait_recv()

    bias_row = bias_v[0:1, :].astype(jnp.float32)
    own_length = lens[replica]
    lane = lax.broadcasted_iota(jnp.int32, (HEAD, HEAD), 1)
    row = lax.broadcasted_iota(jnp.int32, (HEAD, HEAD), 0)
    in_first = lane < HALF

    def finish(i, value):
        part = pl.ds(i * HEAD, HEAD)
        scale = jnp.broadcast_to(inverse[i:i + 1, :], (HEAD, HEAD)).T
        value = value * scale + bias_row
        trig = t_v[part, :]
        swapped = pltpu.roll(trig, HALF, 1)
        cosine = jnp.where(in_first, trig, swapped)
        sine = jnp.where(in_first, -swapped, trig)
        rotated = value * cosine + pltpu.roll(value, HALF, 1) * sine
        kept = jnp.where(row + i * HEAD < own_length, rotated, 0.0)
        out[part, :] = kept.astype(jnp.bfloat16)

    for sub in range(subs):
        value = product(last, sub)
        halves = [incoming(1, True, half, sub) + incoming(1, False, half, sub) for half in (0, 1)]
        total = value + jnp.concatenate(trade(*halves), axis=0)
        for i in range(SUB // HEAD):
            finish(sub * SUB // HEAD + i, total[i * HEAD:(i + 1) * HEAD])

    for copy in started:
        copy.wait_send()
    for distance in range(1, ring):
        square_copy(distance).wait_send()

    @pl.when(slot == 0)
    def _():
        for i in range(ring):
            for copy in head_copies(i):
                copy.wait_send()
        for copy in bias_copies():
            copy.wait_send()

    @pl.when(slot == 2)
    def _():
        for i in range(ring):
            pass_copy(i).wait_send()


def solution(mesh):
    ring = mesh.shape["tensor"]

    def local(hidden, norm_gain, layer_weight, layer_bias, lengths):
        rows, depth = hidden.shape
        subs = rows // SUB
        far = ring // 2
        table = jnp.asarray(rope_table(rows))
        dma = pltpu.SemaphoreType.DMA
        return pl.pallas_call(
            functools.partial(kernel, ring),
            out_shape=jax.ShapeDtypeStruct((rows, HEAD), jnp.bfloat16),
            in_specs=[pl.BlockSpec(memory_space=pl.ANY)] * 6,
            out_specs=pl.BlockSpec(memory_space=pltpu.VMEM),
            scratch_shapes=[
                pltpu.VMEM((rows, depth), jnp.bfloat16),
                pltpu.VMEM((rows, depth), jnp.bfloat16),
                pltpu.VMEM((ring - 2, depth, HEAD), jnp.bfloat16),
                pltpu.VMEM((ring, depth, HEAD), jnp.bfloat16),
                pltpu.VMEM((rows, HEAD), jnp.float32),
                pltpu.VMEM((depth,), jnp.bfloat16),
                pltpu.VMEM((1, HEAD), jnp.bfloat16),
                pltpu.SMEM(lengths.shape, jnp.int32),
                pltpu.VMEM((ring, rows // HEAD, HEAD), jnp.float32),
                pltpu.VMEM((16, HEAD), jnp.bfloat16),
                pltpu.VMEM((2 * far, 2, rows // 2, HEAD), jnp.bfloat16),
                pltpu.VMEM((2 * far, 2, rows // 2, HEAD), jnp.bfloat16),
                dma((subs,)),
                dma,
                dma((3,)),
                dma((ring - 2,)),
                dma((ring,)),
                dma((ring, 2)),
                dma((ring,)),
                dma((ring,)),
                dma((ring,)),
                dma((GROUP,)),
                dma,
                dma((2 * far, 2, subs)),
                dma((2 * far, 2, subs)),
            ],
            compiler_params=pltpu.CompilerParams(
                collective_id=0, has_side_effects=True, vmem_limit_bytes=60 * 1024 * 1024
            ),
            name="keys",
        )(hidden, norm_gain, layer_weight, layer_bias, lengths, table)

    in_specs = (
        P("replica", "tensor"),
        P("tensor"),
        P("replica", "tensor", None),
        P("replica", "tensor"),
        P(),
    )
    return jax.shard_map(
        local, mesh=mesh, in_specs=in_specs, out_specs=P("replica", "tensor"), check_vma=False
    )
```

time: 54.7 us -> 44.4 us (0.81)
  the two profiles are of different devices: /device:TPU:59 before, /device:TPU:47 now
where the time goes in v2:
time: 44.4 us; the launch traced here: 44.2 us
  Pallas kernels  42.5 us (96%)
  local copies, waits for them, and re-layouts  1.67 us (4%)
    pallas_call x1, Pallas kernels, local(): pl.pallas_call(functools.partial(kernel, ring), out_shape=jax.ShapeDtypeS...  42.5 us
    unnamed x1, local copies, waits for them, and re-layouts  1.67 us

profile of v2, /device:TPU:47, one launch (start us, length us, event | category | flops | bytes accessed | tf_op | source)
XLA Modules:
  0.0 44.2 jit_solution(16557168713606669208)
XLA Ops:
  0.0 42.5 %keys.1 = bf16[1024,128]{1,0:T(8,128)(2,1)} custom-call(bf16[1024,1024]{1,0:T(8,128)(2,1)} %hid.1, bf16[1024]{0:T(1024)(128)(2,1)} %gain_h.1, bf16[1,1024,1024]{2,1,0:T(8,128)(2,1)} %weight.1, bf16[1,128]{1,0:T(2,128)(2,1)} %bias_h.1, s32[64]{0:T(128)} %lens_h.1, f32[1024,128]{1,0:T(8,128)} %constant.2.clone.table), custom_call_target="tpu_custom_call" | custom-call | tf_op jit(solution)/shard_map/keys/pallas_call | solution.py:312
  42.5 1.7 %copy.8 = bf16[1024,128]{1,0:T(8,128)(2,1)} copy(bf16[1024,128]{1,0:T(8,128)(2,1)} %keys.1) | data formatting | bytes 524288

commit v3 on v2

--- a/solution.py
+++ b/solution.py
@@ -12,6 +12,7 @@
 HALF = HEAD // 2
 GROUP = 4
 SUB = 512
+MOVED = 128
 EPSILON = 1e-06
 ROPE_BASE = 1000000.0
 MESH = pl.DeviceIdType.MESH
@@ -35,9 +36,9 @@
     ring,
     hid, gain_h, weight, bias_h, lens_h, table,
     out,
-    h_v, n_v, w_n, w_v, t_v, gain, bias, lens, squares, bias_v, send_v, recv_v,
+    h_v, n_v, w_n, w_v, t_v, gain, bias, lens, squares, bias_v, sums_v, moved_v, send_v, recv_v,
     h_sem, t_sem, small_sem, n_sem, w_sem, head_send, pass_send,
-    square_send, square_recv, bias_send, bias_recv, ring_send, ring_recv,
+    square_send, square_recv, bias_send, bias_recv, move_sem, back_sem, ring_send, ring_recv,
 ):
     rows, depth = h_v.shape
     subs = rows // SUB
@@ -133,10 +134,9 @@
             for step in range(1, GROUP)
         ]
 
-    def prepare():
-        load_gain.wait()
+    def prepare(blocks):
         gain_row = gain[...].astype(jnp.float32).reshape(1, depth)
-        for block in range(subs):
+        for block in blocks:
             load_hidden(block).wait()
             for i in range(block * SUB // HEAD, (block + 1) * SUB // HEAD):
                 part = pl.ds(i * HEAD, HEAD)
@@ -148,24 +148,53 @@
                     n_v[part, cols] = (piece * gain_row[:, cols]).astype(jnp.bfloat16)
                 squares[0, pl.ds(i, 1), :] = jnp.sum(total.T, axis=0, keepdims=True)
 
-    @pl.when(slot == 0)
-    def _():
-        load_whole(0).wait()
-        mix(far - 1)
-        pl.semaphore_wait(barrier, waits)
-        for i in range(ring):
-            if i > 2 and i < last and i % 2 == 1:
+    kept = rows - MOVED
+    other = head + lax.rem(slot + 2, GROUP)
+
+    def move_copy():
+        return pltpu.make_async_remote_copy(
+            src_ref=n_v.at[pl.ds(kept, MOVED)], dst_ref=n_v.at[pl.ds(rows, MOVED)],
+            send_sem=move_sem.at[0], recv_sem=move_sem.at[1],
+            device_id={"replica": other}, device_id_type=MESH)
+
+    def back_copy():
+        return pltpu.make_async_remote_copy(
+            src_ref=moved_v, dst_ref=sums_v.at[pl.ds(kept, MOVED)],
+            send_sem=back_sem.at[0], recv_sem=back_sem.at[1],
+            device_id={"replica": other}, device_id_type=MESH)
+
+    def send_weight(blocks):
+        for i in blocks:
+            if 2 < i < last and i % 2 == 1:
                 mix(far - 1 - i // 2)
             if i == last:
                 load_whole(last).wait()
             for copy in head_copies(i):
                 copy.start()
-        prepare()
-
-    @pl.when(slot > 0)
-    def _():
-        prepare()
+
+    load_gain.wait()
+    early = range(subs // 2)
+    late = range(subs // 2, subs)
+
+    @pl.when(slot == 0)
+    def _():
+        load_whole(0).wait()
+        mix(far - 1)
         pl.semaphore_wait(barrier, waits)
+        send_weight(range(ring))
+        prepare(range(subs))
+
+    @pl.when(slot == 1)
+    def _():
+        prepare(range(subs))
+        pl.semaphore_wait(barrier, waits)
+
+    @pl.when(slot > 1)
+    def _():
+        prepare(late)
+        pl.semaphore_wait(barrier, waits)
+        move_copy().start()
+        prepare(early)
 
     def square_copy(distance):
         return pltpu.make_async_remote_copy(
@@ -192,78 +221,95 @@
         def _():
             pass_copy(i).start()
 
-    def product(i, sub):
-        return jnp.dot(n_v[pl.ds(sub * SUB, SUB), :], w_v[i], preferred_element_type=jnp.float32)
-
-    def ring_copy(distance, positive, half, sub):
-        h = (distance - 1) + (0 if positive else far)
-        part = pl.ds(sub * SUB // 2, SUB // 2)
-        return pltpu.make_async_remote_copy(
-            src_ref=send_v.at[h, half, part], dst_ref=recv_v.at[h, half, part],
-            send_sem=ring_send.at[h, half, sub], recv_sem=ring_recv.at[h, half, sub],
-            device_id={"tensor": at(1 if positive else -1)}, device_id_type=MESH)
-
-    def incoming(distance, positive, half, sub):
-        ring_copy(distance, positive, half, sub).wait_recv()
-        h = (distance - 1) + (0 if positive else far)
-        return recv_v[h, half, pl.ds(sub * SUB // 2, SUB // 2)].astype(jnp.float32)
-
-    started = []
-
-    def forward(distance, positive, half, sub, value):
-        h = (distance - 1) + (0 if positive else far)
-        send_v[h, half, pl.ds(sub * SUB // 2, SUB // 2)] = value.astype(jnp.bfloat16)
-        copy = ring_copy(distance, positive, half, sub)
-        copy.start()
-        started.append(copy)
-
-    def starts(positive, sub):
-        return (sub < subs // 2) == positive
-
-    take_weight(0)
-    for sub in range(subs):
-        value = product(0, sub)
-        for half, packed in enumerate(trade(value[:SUB // 2], value[SUB // 2:])):
-            forward(far, starts(True, sub), half, sub, packed)
-
-    for k in range(far - 1, 0, -1):
-        for half in (0, 1):
-            take_weight(block_of(k, half))
-            for sub in range(subs):
-                value = product(block_of(k, half), sub)
-                plus, minus = trade(value[:SUB // 2], value[SUB // 2:])
-                ways = [(True, plus), (False, minus)]
-                if k == far - 1 and starts(True, sub):
-                    ways = ways[::-1]
-                for positive, packed in ways:
-                    if k < far - 1 or starts(positive, sub):
-                        packed = packed + incoming(k + 1, positive, half, sub)
-                    forward(k, positive, half, sub, packed)
-
-    take_weight(last)
-    load_table.wait()
-    load_lens.wait()
-    sums = squares[0]
-    for distance in range(1, ring):
-        square_copy(distance).wait_recv()
-        sums = sums + squares[distance]
-    inverse = lax.rsqrt(sums / (depth * ring) + EPSILON)
-
-    @pl.when(slot > 0)
-    def _():
-        pltpu.make_async_remote_copy(
-            src_ref=bias_v, dst_ref=bias_v,
-            send_sem=bias_send.at[1], recv_sem=bias_recv,
-            device_id={"replica": head}, device_id_type=MESH).wait_recv()
-
-    bias_row = bias_v[0:1, :].astype(jnp.float32)
-    own_length = lens[replica]
-    lane = lax.broadcasted_iota(jnp.int32, (HEAD, HEAD), 1)
-    row = lax.broadcasted_iota(jnp.int32, (HEAD, HEAD), 0)
-    in_first = lane < HALF
-
-    def finish(i, value):
+    inside_a = [(0, rows // 2), (rows // 2, rows // 2), (rows, MOVED)]
+    inside_b = [(0, kept // 2), (kept // 2, kept // 2)]
+
+    def product(i, rows_of):
+        start, size = rows_of
+        return jnp.dot(n_v[pl.ds(start, size), :], w_v[i], preferred_element_type=jnp.float32)
+
+    def trade_rows(value):
+        size = value.shape[0] // 2
+        return trade(value[:size], value[size:])
+
+    def hop(distance, positive):
+        return (distance - 1) + (0 if positive else far)
+
+    def starts(positive, seg, half):
+        return ((seg, half) in ((0, 0), (0, 1), (2, 0))) == positive
+
+    def ring_pass(segments):
+        def ring_copy(distance, positive, half, seg):
+            h = hop(distance, positive)
+            start, size = segments[seg]
+            part = pl.ds(start // 2, size // 2)
+            return pltpu.make_async_remote_copy(
+                src_ref=send_v.at[h, half, part], dst_ref=recv_v.at[h, half, part],
+                send_sem=ring_send.at[h, half, seg], recv_sem=ring_recv.at[h, half, seg],
+                device_id={"tensor": at(1 if positive else -1)}, device_id_type=MESH)
+
+        def incoming(distance, positive, half, seg):
+            ring_copy(distance, positive, half, seg).wait_recv()
+            start, size = segments[seg]
+            return recv_v[hop(distance, positive), half, pl.ds(start // 2, size // 2)].astype(jnp.float32)
+
+        started = []
+
+        def forward(distance, positive, half, seg, value):
+            start, size = segments[seg]
+            send_v[hop(distance, positive), half, pl.ds(start // 2, size // 2)] = value.astype(jnp.bfloat16)
+            copy = ring_copy(distance, positive, half, seg)
+            copy.start()
+            started.append(copy)
+
+        def stage(i, seg):
+            value = trade_rows(product(i, segments[seg]))
+            if i == 0:
+                for half, packed in enumerate(value):
+                    forward(far, starts(True, seg, half), half, seg, packed)
+                return
+            k, half = far - 1 - (i - 1) // 2, (i - 1) % 2
+            ways = [(True, value[0]), (False, value[1])]
+            if k == far - 1 and starts(True, seg, half):
+                ways = ways[::-1]
+            for positive, packed in ways:
+                if k < far - 1 or starts(positive, seg, half):
+                    packed = packed + incoming(k + 1, positive, half, seg)
+                forward(k, positive, half, seg, packed)
+
+        def total(seg):
+            value = product(last, segments[seg])
+            halves = [incoming(1, True, half, seg) + incoming(1, False, half, seg) for half in (0, 1)]
+            return value + jnp.concatenate(trade(*halves), axis=0)
+
+        def drain():
+            for copy in started:
+                copy.wait_send()
+
+        return stage, total, drain
+
+    def ready():
+        load_table.wait()
+        load_lens.wait()
+        sums = squares[0]
+        for distance in range(1, ring):
+            square_copy(distance).wait_recv()
+            sums = sums + squares[distance]
+
+        @pl.when(slot > 0)
+        def _():
+            pltpu.make_async_remote_copy(
+                src_ref=bias_v, dst_ref=bias_v,
+                send_sem=bias_send.at[1], recv_sem=bias_recv,
+                device_id={"replica": head}, device_id_type=MESH).wait_recv()
+
+        return lax.rsqrt(sums / (depth * ring) + EPSILON), bias_v[0:1, :].astype(jnp.float32)
+
+    def finish(i, value, inverse, bias_row):
         part = pl.ds(i * HEAD, HEAD)
+        lane = lax.broadcasted_iota(jnp.int32, (HEAD, HEAD), 1)
+        row = lax.broadcasted_iota(jnp.int32, (HEAD, HEAD), 0)
+        in_first = lane < HALF
         scale = jnp.broadcast_to(inverse[i:i + 1, :], (HEAD, HEAD)).T
         value = value * scale + bias_row
         trig = t_v[part, :]
@@ -271,18 +317,55 @@
         cosine = jnp.where(in_first, trig, swapped)
         sine = jnp.where(in_first, -swapped, trig)
         rotated = value * cosine + pltpu.roll(value, HALF, 1) * sine
-        kept = jnp.where(row + i * HEAD < own_length, rotated, 0.0)
-        out[part, :] = kept.astype(jnp.bfloat16)
-
-    for sub in range(subs):
-        value = product(last, sub)
-        halves = [incoming(1, True, half, sub) + incoming(1, False, half, sub) for half in (0, 1)]
-        total = value + jnp.concatenate(trade(*halves), axis=0)
-        for i in range(SUB // HEAD):
-            finish(sub * SUB // HEAD + i, total[i * HEAD:(i + 1) * HEAD])
-
-    for copy in started:
-        copy.wait_send()
+        masked = jnp.where(row + i * HEAD < lens[replica], rotated, 0.0)
+        out[part, :] = masked.astype(jnp.bfloat16)
+
+    moved_at = {2: [0], 3: [1, 2], 4: [3, 4], 5: [5], 6: [6]}
+
+    @pl.when(slot < 2)
+    def _():
+        stage, total, drain = ring_pass(inside_a)
+        for i in range(last):
+            take_weight(i)
+            if i == min(moved_at):
+                move_copy().wait_recv()
+            for j in moved_at.get(i, []):
+                stage(j, 2)
+            for seg in (0, 1):
+                stage(i, seg)
+        take_weight(last)
+        moved_v[...] = total(2)
+        back_copy().start()
+        inverse, bias_row = ready()
+        for seg in (0, 1):
+            value = total(seg)
+            start, size = inside_a[seg]
+            for r in range(0, size, HEAD):
+                finish((start + r) // HEAD, value[r:r + HEAD], inverse, bias_row)
+        drain()
+        back_copy().wait_send()
+
+    @pl.when(slot > 1)
+    def _():
+        stage, total, drain = ring_pass(inside_b)
+        for i in range(last):
+            take_weight(i)
+            for seg in (0, 1):
+                stage(i, seg)
+        take_weight(last)
+        inverse, bias_row = ready()
+        done = 0
+        for seg, (start, size) in enumerate(inside_b):
+            sums_v[pl.ds(start, size), :] = total(seg)
+            for i in range(done, (start + size) // HEAD):
+                finish(i, sums_v[pl.ds(i * HEAD, HEAD), :], inverse, bias_row)
+            done = (start + size) // HEAD
+        back_copy().wait_recv()
+        for i in range(done, rows // HEAD):
+            finish(i, sums_v[pl.ds(i * HEAD, HEAD), :], inverse, bias_row)
+        drain()
+        move_copy().wait_send()
+
     for distance in range(1, ring):
         square_copy(distance).wait_send()
 
@@ -309,6 +392,7 @@
         far = ring // 2
         table = jnp.asarray(rope_table(rows))
         dma = pltpu.SemaphoreType.DMA
+        arrays = (hidden, norm_gain, layer_weight, layer_bias, lengths, table)
         return pl.pallas_call(
             functools.partial(kernel, ring),
             out_shape=jax.ShapeDtypeStruct((rows, HEAD), jnp.bfloat16),
@@ -316,7 +400,7 @@
             out_specs=pl.BlockSpec(memory_space=pltpu.VMEM),
             scratch_shapes=[
                 pltpu.VMEM((rows, depth), jnp.bfloat16),
-                pltpu.VMEM((rows, depth), jnp.bfloat16),
+                pltpu.VMEM((rows + MOVED, depth), jnp.bfloat16),
                 pltpu.VMEM((ring - 2, depth, HEAD), jnp.bfloat16),
                 pltpu.VMEM((ring, depth, HEAD), jnp.bfloat16),
                 pltpu.VMEM((rows, HEAD), jnp.float32),
@@ -325,8 +409,10 @@
                 pltpu.SMEM(lengths.shape, jnp.int32),
                 pltpu.VMEM((ring, rows // HEAD, HEAD), jnp.float32),
                 pltpu.VMEM((16, HEAD), jnp.bfloat16),
-                pltpu.VMEM((2 * far, 2, rows // 2, HEAD), jnp.bfloat16),
-                pltpu.VMEM((2 * far, 2, rows // 2, HEAD), jnp.bfloat16),
+                pltpu.VMEM((rows, HEAD), jnp.float32),
+                pltpu.VMEM((MOVED, HEAD), jnp.float32),
+                pltpu.VMEM((2 * far, 2, (rows + MOVED) // 2, HEAD), jnp.bfloat16),
+                pltpu.VMEM((2 * far, 2, (rows + MOVED) // 2, HEAD), jnp.bfloat16),
                 dma((subs,)),
                 dma,
                 dma((3,)),
@@ -338,14 +424,16 @@
                 dma((ring,)),
                 dma((GROUP,)),
                 dma,
-                dma((2 * far, 2, subs)),
-                dma((2 * far, 2, subs)),
+                dma((2,)),
+                dma((2,)),
+                dma((2 * far, 2, 3)),
+                dma((2 * far, 2, 3)),
             ],
             compiler_params=pltpu.CompilerParams(
-                collective_id=0, has_side_effects=True, vmem_limit_bytes=60 * 1024 * 1024
+                collective_id=0, has_side_effects=True, vmem_limit_bytes=48 * 1024 * 1024
             ),
             name="keys",
-        )(hidden, norm_gain, layer_weight, layer_bias, lengths, table)
+        )(*(pltpu.with_memory_space_constraint(x, pltpu.HBM) for x in arrays))
 
     in_specs = (
         P("replica", "tensor"),

time: 44.4 us -> 42.3 us (0.953)
  Pallas kernels: 42.5 us -> 41.4 us
  local copies, waits for them, and re-layouts: 1.67 us -> 0.71 us
    pallas_call x1, Pallas kernels: 42.5 us -> 41.4 us  [local(): pl.pallas_call(functools.partial(kernel, ring), out_shape=jax.ShapeDtypeS...]
    unnamed x1, local copies, waits for them, and re-layouts: 1.67 us -> 0.71 us
where the time goes in v3:
time: 42.3 us; the launch traced here: 42.1 us
  Pallas kernels  41.4 us (98%)
  local copies, waits for them, and re-layouts  0.71 us (2%)
    pallas_call x1, Pallas kernels, local(): pl.pallas_call(functools.partial(kernel, ring), out_shape=jax.ShapeDtypeS...  41.4 us

profile of v3, /device:TPU:47, one launch (start us, length us, event | category | flops | bytes accessed | tf_op | source)
XLA Modules:
  0.0 42.1 jit_solution(9925083672540475869)
XLA Ops:
  0.0 41.4 %keys.1 = bf16[1024,128]{1,0:T(8,128)(2,1)S(1)} custom-call(bf16[1024,1024]{1,0:T(8,128)(2,1)} %hid.1, bf16[1024]{0:T(1024)(128)(2,1)} %gain_h.1, bf16[1,1024,1024]{2,1,0:T(8,128)(2,1)} %weight.1, bf16[1,128]{1,0:T(2,128)(2,1)} %bias_h.1, s32[64]{0:T(128)} %lens_h.1, f32[1024,128]{1,0:T(8,128)} %constant.2.clone.table), custom_call_target="tpu_custom_call" | custom-call | tf_op jit(solution)/shard_map/keys/pallas_call | solution.py:396
  41.4 0.7 %copy.8 = bf16[1024,128]{1,0:T(8,128)(2,1)} copy(bf16[1024,128]{1,0:T(8,128)(2,1)S(1)} %keys.1) | data formatting | bytes 524288

commit v4 on v3

--- a/solution.py
+++ b/solution.py
@@ -12,7 +12,8 @@
 HALF = HEAD // 2
 GROUP = 4
 SUB = 512
-MOVED = 128
+MOVED = 64
+READY_AFTER = 4
 EPSILON = 1e-06
 ROPE_BASE = 1000000.0
 MESH = pl.DeviceIdType.MESH
@@ -36,7 +37,7 @@
     ring,
     hid, gain_h, weight, bias_h, lens_h, table,
     out,
-    h_v, n_v, w_n, w_v, t_v, gain, bias, lens, squares, bias_v, sums_v, moved_v, send_v, recv_v,
+    h_v, n_v, w_n, w_v, t_v, gain, bias, lens, squares, bias_v, sums_v, moved_v, turn_v, send_v, recv_v,
     h_sem, t_sem, small_sem, n_sem, w_sem, head_send, pass_send,
     square_send, square_recv, bias_send, bias_recv, move_sem, back_sem, ring_send, ring_recv,
 ):
@@ -173,6 +174,7 @@
                 copy.start()
 
     load_gain.wait()
+    load_bias.wait()
     early = range(subs // 2)
     late = range(subs // 2, subs)
 
@@ -180,7 +182,10 @@
     def _():
         load_whole(0).wait()
         mix(far - 1)
+        bias_v[...] = jnp.broadcast_to(bias[...], bias_v.shape)
         pl.semaphore_wait(barrier, waits)
+        for copy in bias_copies():
+            copy.start()
         send_weight(range(ring))
         prepare(range(subs))
 
@@ -204,14 +209,6 @@
 
     for distance in range(1, ring):
         square_copy(distance).start()
-    load_bias.wait()
-
-    @pl.when(slot == 0)
-    def _():
-        bias_v[...] = jnp.broadcast_to(bias[...], bias_v.shape)
-        for copy in bias_copies():
-            copy.start()
-
     def take_weight(i):
         @pl.when(slot > 0)
         def _():
@@ -222,7 +219,7 @@
             pass_copy(i).start()
 
     inside_a = [(0, rows // 2), (rows // 2, rows // 2), (rows, MOVED)]
-    inside_b = [(0, kept // 2), (kept // 2, kept // 2)]
+    inside_b = [(start, min(rows // 4, kept - start)) for start in range(0, kept, rows // 4)]
 
     def product(i, rows_of):
         start, size = rows_of
@@ -235,10 +232,12 @@
     def hop(distance, positive):
         return (distance - 1) + (0 if positive else far)
 
-    def starts(positive, seg, half):
-        return ((seg, half) in ((0, 0), (0, 1), (2, 0))) == positive
-
     def ring_pass(segments):
+        def starts(positive, seg, half):
+            if segments[seg][0] == rows:
+                return (half == 0) == positive
+            return (segments[seg][0] < rows // 2) == positive
+
         def ring_copy(distance, positive, half, seg):
             h = hop(distance, positive)
             start, size = segments[seg]
@@ -303,20 +302,25 @@
                 send_sem=bias_send.at[1], recv_sem=bias_recv,
                 device_id={"replica": head}, device_id_type=MESH).wait_recv()
 
-        return lax.rsqrt(sums / (depth * ring) + EPSILON), bias_v[0:1, :].astype(jnp.float32)
-
-    def finish(i, value, inverse, bias_row):
+        inverse = lax.rsqrt(sums / (depth * ring) + EPSILON)
+        bias_rows = jnp.broadcast_to(bias_v[0:1, :].astype(jnp.float32), (HEAD, HEAD))
+        bias_other = pltpu.roll(bias_rows, HALF, 1)
+        in_first = lax.broadcasted_iota(jnp.int32, (HEAD, HEAD), 1) < HALF
+        for i in range(rows // HEAD):
+            part = pl.ds(i * HEAD, HEAD)
+            scale = jnp.broadcast_to(inverse[i:i + 1, :], (HEAD, HEAD)).T
+            trig = t_v[part, :]
+            swapped = pltpu.roll(trig, HALF, 1)
+            cosine = jnp.where(in_first, trig, swapped)
+            sine = jnp.where(in_first, -swapped, trig)
+            turn_v[0, part, :] = scale * cosine
+            turn_v[1, part, :] = scale * sine
+            turn_v[2, part, :] = bias_rows * cosine + bias_other * sine
+
+    def finish(i, value):
         part = pl.ds(i * HEAD, HEAD)
-        lane = lax.broadcasted_iota(jnp.int32, (HEAD, HEAD), 1)
         row = lax.broadcasted_iota(jnp.int32, (HEAD, HEAD), 0)
-        in_first = lane < HALF
-        scale = jnp.broadcast_to(inverse[i:i + 1, :], (HEAD, HEAD)).T
-        value = value * scale + bias_row
-        trig = t_v[part, :]
-        swapped = pltpu.roll(trig, HALF, 1)
-        cosine = jnp.where(in_first, trig, swapped)
-        sine = jnp.where(in_first, -swapped, trig)
-        rotated = value * cosine + pltpu.roll(value, HALF, 1) * sine
+        rotated = value * turn_v[0, part, :] + pltpu.roll(value, HALF, 1) * turn_v[1, part, :] + turn_v[2, part, :]
         masked = jnp.where(row + i * HEAD < lens[replica], rotated, 0.0)
         out[part, :] = masked.astype(jnp.bfloat16)
 
@@ -333,15 +337,16 @@
                 stage(j, 2)
             for seg in (0, 1):
                 stage(i, seg)
+            if i == READY_AFTER:
+                ready()
         take_weight(last)
         moved_v[...] = total(2)
         back_copy().start()
-        inverse, bias_row = ready()
         for seg in (0, 1):
             value = total(seg)
             start, size = inside_a[seg]
             for r in range(0, size, HEAD):
-                finish((start + r) // HEAD, value[r:r + HEAD], inverse, bias_row)
+                finish((start + r) // HEAD, value[r:r + HEAD])
         drain()
         back_copy().wait_send()
 
@@ -350,19 +355,20 @@
         stage, total, drain = ring_pass(inside_b)
         for i in range(last):
             take_weight(i)
-            for seg in (0, 1):
+            for seg in range(len(inside_b)):
                 stage(i, seg)
+            if i == READY_AFTER:
+                ready()
         take_weight(last)
-        inverse, bias_row = ready()
         done = 0
         for seg, (start, size) in enumerate(inside_b):
             sums_v[pl.ds(start, size), :] = total(seg)
             for i in range(done, (start + size) // HEAD):
-                finish(i, sums_v[pl.ds(i * HEAD, HEAD), :], inverse, bias_row)
+                finish(i, sums_v[pl.ds(i * HEAD, HEAD), :])
             done = (start + size) // HEAD
         back_copy().wait_recv()
         for i in range(done, rows // HEAD):
-            finish(i, sums_v[pl.ds(i * HEAD, HEAD), :], inverse, bias_row)
+            finish(i, sums_v[pl.ds(i * HEAD, HEAD), :])
         drain()
         move_copy().wait_send()
 
@@ -411,6 +417,7 @@
                 pltpu.VMEM((16, HEAD), jnp.bfloat16),
                 pltpu.VMEM((rows, HEAD), jnp.float32),
                 pltpu.VMEM((MOVED, HEAD), jnp.float32),
+                pltpu.VMEM((3, rows, HEAD), jnp.float32),
                 pltpu.VMEM((2 * far, 2, (rows + MOVED) // 2, HEAD), jnp.bfloat16),
                 pltpu.VMEM((2 * far, 2, (rows + MOVED) // 2, HEAD), jnp.bfloat16),
                 dma((subs,)),
@@ -426,8 +433,8 @@
                 dma,
                 dma((2,)),
                 dma((2,)),
-                dma((2 * far, 2, 3)),
-                dma((2 * far, 2, 3)),
+                dma((2 * far, 2, 4)),
+                dma((2 * far, 2, 4)),
             ],
             compiler_params=pltpu.CompilerParams(
                 collective_id=0, has_side_effects=True, vmem_limit_bytes=48 * 1024 * 1024

time: 42.3 us -> 42.3 us (level)
  the two profiles are of different devices: /device:TPU:47 before, /device:TPU:63 now
where the time goes in v4:
time: 42.3 us; the launch traced here: 42.2 us
  Pallas kernels  41.4 us (98%)
  local copies, waits for them, and re-layouts  0.71 us (2%)
    pallas_call x1, Pallas kernels, local(): pl.pallas_call(functools.partial(kernel, ring), out_shape=jax.ShapeDtypeS...  41.4 us

profile of v4, /device:TPU:63, one launch (start us, length us, event | category | flops | bytes accessed | tf_op | source)
XLA Modules:
  0.0 42.2 jit_solution(2214740454509213103)
XLA Ops:
  0.0 41.4 %keys.1 = bf16[1024,128]{1,0:T(8,128)(2,1)S(1)} custom-call(bf16[1024,1024]{1,0:T(8,128)(2,1)} %hid.1, bf16[1024]{0:T(1024)(128)(2,1)} %gain_h.1, bf16[1,1024,1024]{2,1,0:T(8,128)(2,1)} %weight.1, bf16[1,128]{1,0:T(2,128)(2,1)} %bias_h.1, s32[64]{0:T(128)} %lens_h.1, f32[1024,128]{1,0:T(8,128)} %constant.2.clone.table), custom_call_target="tpu_custom_call" | custom-call | tf_op jit(solution)/shard_map/keys/pallas_call | solution.py:402
  41.4 0.7 %copy.8 = bf16[1024,128]{1,0:T(8,128)(2,1)} copy(bf16[1024,128]{1,0:T(8,128)(2,1)S(1)} %keys.1) | data formatting | bytes 524288
